TPU v7x, 256 devices: a whole 4x4x8 slice. The times are simulated.
256 devices in a mesh: chan: 32 (over z, x_hi, core), band: 8 (over y, x_lo).
Axes of the slice: x: 4 (x_hi: 2, x_lo: 2; x = x_hi * 2 + x_lo), y: 4, z: 8, core: 2. Of those that a mesh axis runs over, the one named last changes fastest.
Arguments:
- spectra: bfloat16 [1024, 128, 1152], P('chan', 'band'), parts along dimension 1, may hold values from -6 to 6
- weights: float32 [128, 1152], P('band'), parts along dimension 0, may hold values from 0.1 to 10
Outputs:
- cross_power: bfloat16 [128, 1024, 1024], P('band', 'chan'), parts along dimension 0
There are 8 independent parts, one for each index of `band`. A program takes and returns all parts, laid end to end along the dimension named above; each array names one. Nothing has to cross between parts.
All inputs are finite; a program needn't handle non-finite values.
Results may differ from a plain program's by a relative error of at most 0.009.
Values may be sent and summed in bfloat16 or wider, within the bound.
A program may use at most 128 MiB of HBM per device.

v0:
```python
import jax
import jax.numpy as jnp
from jax import lax
from jax.sharding import PartitionSpec as P


def cross_tile(weighted, coeffs):
    return jnp.einsum("clm,dlm->lcd", weighted, coeffs, preferred_element_type=jnp.float32).astype(
        jnp.bfloat16
    )


def per_device(spectra, weights):
    weight_sum = jnp.sum(weights, axis=1)
    scaled = weights / weight_sum[:, None]
    weighted = (spectra.astype(jnp.float32) * scaled[None, :, :]).astype(jnp.bfloat16)
    return cross_tile(weighted, lax.all_gather(spectra, "chan", axis=0, tiled=True))


def solution(mesh):
    placed = (P("chan", "band", None), P("band", None))
    return jax.shard_map(
        per_device, mesh=mesh, in_specs=placed, out_specs=P("band", "chan", None), check_vma=False
    )
```

profile of v0, /device:TPU:1, one launch (start us, length us, event | category | flops | bytes accessed | tf_op | source)
XLA Modules:
  0.0 291.0 jit_solution(1529174530005182986)
XLA Ops:
  6.5 0.0 all-gather.2.cloned.1.call-start
  6.5 0.0 copy-start.1
  6.5 2.5 copy.3
  9.1 0.0 copy-start
  9.1 0.0 all-gather.2.cloned.1.call-update
  9.1 0.0 copy-done.1
  9.1 0.1 reduce_sum.9
  9.2 0.1 broadcast_divide_fusion
  9.3 1.0 copy-done
  10.3 0.2 multiply_convert_fusion
  10.5 255.3 %all-gather.2.cloned.1.call-done = bf16[1024,16,1152]{2,0,1:T(8,128)(2,1)} async-done(((bf16[32,16,1152]{2,0,1:T(8,128)(2,1)}), bf16[1024,16,1152]{2,0,1:T(8,128)(2,1)}) %all-gather.2.cloned.1.call-update) | async-done | bytes 37748752 | tf_op jit(solution)/shard_map/all_gather | solution.py:17
  265.9 18.2 %convolution_convert_fusion = bf16[16,32,1024]{2,1,0:T(8,128)(2,1)} fusion(bf16[1024,16,1152]{2,0,1:T(8,128)(2,1)} %all-gather.2.cloned.1.call-done, bf16[32,16,1152]{2,1,0:T(8,128)(2,1)S(1)} %multiply_convert_fusion), kind=kOutput, calls=%fused_computation.1 | convolution fusion | flops 1208483840 | bytes 39976960 | tf_op jit(solution)/shard_map/clm,dlm->lcd/dot_general | solution.py:8
Async XLA Ops:
  6.5 259.3 %all-gather.2.cloned.1.call-start = ((), (), s32[]{:S(2)}) async-start(), calls=%async_computation | async-start | bytes 38928384 | tf_op jit(solution)/shard_map/all_gather | solution.py:17
  6.5 2.6 copy-start.1
  9.1 1.3 copy-start
Sparse Core Ops, SparseCore 0:
  10.2 255.6 all-gather.1
where the time goes:
time: 291 us
  waiting for transfers between devices  255 us (88%)
  matrix products  18.2 us (6%)
  between operations  13.4 us (5%)
  local copies, waits for them, and re-layouts  3.56 us (1%)
    all_gather x1, waiting for transfers between devices, per_device(): lax.all_gather(spectra, 'chan', axis=0, tiled=True)  255 us
    dot_general x1, matrix products, cross_tile(): jnp.einsum('clm,dlm->lcd', weighted, coeffs, preferred_element_type=jnp.f...  18.2 us
  transfers between devices with their start and end apart: 1, of which 1 were waited for; matrix products, arithmetic and copies ran while one was open for 0% of the time, Pallas kernels for 0%

commit v1 on v0

v1 whole, which is shorter than its diff:
```python
import functools

import jax
import jax.numpy as jnp
from jax import lax
from jax.experimental import pallas as pl
from jax.experimental.pallas import tpu as pltpu
from jax.sharding import PartitionSpec as P

MESH = pl.DeviceIdType.MESH
BF16 = jnp.bfloat16
F32 = jnp.float32

ZS = 8
OWN = 32
BANDL = 16
ML = 1152
CH = 1024


def step_of(t):
    u, dc = t // 2, t % 2
    mag = 4 - (u + 1) // 2
    return jnp.where(u % 2 == 1, mag, 8 - mag) % 8, dc


def kernel(
    x_ref, w_ref, o_ref, send, full, left, stage, s1, r1, s2, r2, s3, r3, own_sem
):
    k = lax.axis_index("chan")
    core, xh, z = k % 2, (k // 2) % 2, k // 4
    me = 2 * z + core

    def chan(zz, xx, cc):
        return (zz * 2 + xx) * 2 + cc

    def to(t):
        dz, dc = step_of(t)
        return (z + dz) % 8, (core + dc) % 2

    def source(t):
        dz, dc = step_of(t)
        return (z + 8 - dz) % 8, (core + dc) % 2

    partner = chan(z, 1 - xh, core)
    barrier = pltpu.get_barrier_semaphore()

    def greet(t, carry):
        zz, cc = source(t)
        pl.semaphore_signal(
            barrier, inc=1, device_id={"chan": chan(zz, xh, cc)}, device_id_type=MESH
        )
        return carry

    lax.fori_loop(0, 14, greet, 0)
    greet(15, 0)
    pl.semaphore_signal(barrier, inc=1, device_id={"chan": partner}, device_id_type=MESH)

    for j in range(ML // 128):
        cols = pl.ds(j * 128, 128)
        send[:, :, cols] = jnp.swapaxes(x_ref[:, :, cols], 0, 1)

    pl.semaphore_wait(barrier, 16)

    def rows(kk):
        return pl.ds(pl.multiple_of(kk * OWN, OWN), OWN)

    def first(t):
        zz, cc = to(t)
        return pltpu.make_async_remote_copy(
            src_ref=send.at[2 * zz + cc],
            dst_ref=full.at[rows(k)],
            send_sem=s1.at[t],
            recv_sem=r1.at[t],
            device_id={"chan": chan(zz, xh, cc)},
            device_id_type=MESH,
        )

    def across(t):
        zz, cc = source(t)
        block = full.at[rows(chan(zz, xh, cc))]
        return pltpu.make_async_remote_copy(
            src_ref=block,
            dst_ref=block,
            send_sem=s2.at[t],
            recv_sem=r2.at[t],
            device_id={"chan": partner},
            device_id_type=MESH,
        )

    def start_first(t, carry):
        first(t).start()
        return carry

    lax.fori_loop(0, 14, start_first, 0)
    start_first(15, 0)
    full[rows(k), :] = send[me]
    across(14).start()

    def forward(t, carry):
        first(t).wait_recv()
        across(t).start()
        return carry

    lax.fori_loop(0, 14, forward, 0)
    forward(15, 0)

    weight = w_ref[pl.ds(me, 1), :]
    scaled = weight / jnp.sum(weight, axis=1, keepdims=True)

    def arrived(t, carry):
        across(t).wait_recv()
        return carry

    lax.fori_loop(0, 16, arrived, 0)

    def back(t):
        zz, cc = to(t)
        return pltpu.make_async_remote_copy(
            src_ref=stage.at[t],
            dst_ref=o_ref.at[me],
            send_sem=s3.at[t],
            recv_sem=r3.at[t],
            device_id={"chan": chan(zz, xh, cc)},
            device_id_type=MESH,
        )

    def chunk(u, last):
        for a in range(4):
            zz, cc = to(4 * u + a)
            block = full[rows(chan(zz, xh, cc)), :].astype(F32)
            left[pl.ds(a * OWN, OWN), :] = (block * scaled).astype(BF16)
        for n in range(CH // 256):
            tile = lax.dot_general(
                left[...],
                full[pl.ds(n * 256, 256), :],
                (((1,), (1,)), ((), ())),
                preferred_element_type=F32,
            ).astype(BF16)
            for a in range(4):
                stage[4 * u + a, :, pl.ds(n * 256, 256)] = tile[a * OWN : (a + 1) * OWN]
        for a in range(4):
            if not (last and a == 2):
                back(4 * u + a).start()

    def chunk_step(u, carry):
        chunk(u, False)
        return carry

    lax.fori_loop(0, 3, chunk_step, 0)
    chunk(3, True)
    own = pltpu.make_async_copy(stage.at[14], o_ref.at[me], own_sem)
    own.start()

    def finish(t, carry):
        first(t).wait_send()
        back(t).wait()
        return carry

    lax.fori_loop(0, 14, finish, 0)
    finish(15, 0)

    def sent(t, carry):
        across(t).wait_send()
        return carry

    lax.fori_loop(0, 16, sent, 0)
    own.wait()


def per_device(spectra, weights):
    return pl.pallas_call(
        kernel,
        out_shape=jax.ShapeDtypeStruct((BANDL, OWN, CH), BF16),
        in_specs=[pl.BlockSpec(memory_space=pltpu.VMEM)] * 2,
        out_specs=pl.BlockSpec(memory_space=pl.ANY),
        scratch_shapes=[
            pltpu.VMEM((BANDL, OWN, ML), BF16),
            pltpu.VMEM((CH, ML), BF16),
            pltpu.VMEM((4 * OWN, ML), BF16),
            pltpu.VMEM((BANDL, OWN, CH), BF16),
        ]
        + [pltpu.SemaphoreType.DMA((16,))] * 6
        + [pltpu.SemaphoreType.DMA],
        compiler_params=pltpu.CompilerParams(
            collective_id=0, has_side_effects=True, vmem_limit_bytes=32 << 20
        ),
        cost_estimate=pl.CostEstimate(
            flops=2 * BANDL * OWN * CH * ML, bytes_accessed=4 << 20, transcendentals=0
        ),
        name="cross",
    )(spectra, weights)


def solution(mesh):
    placed = (P("chan", "band", None), P("band", None))
    return jax.shard_map(
        per_device, mesh=mesh, in_specs=placed, out_specs=P("band", "chan", None), check_vma=False
    )
```

time: 291 us -> 79.4 us (0.27)
  waiting for transfers between devices: 255 us -> 0 us
  Pallas kernels: 0 us -> 76.1 us
  matrix products: 18.2 us -> 0 us
  between operations: 13.4 us -> 0.01 us
    all_gather x1 -> x0, waiting for transfers between devices: 255 us -> none  [per_device(): lax.all_gather(spectra, 'chan', axis=0, tiled=True)]
    pallas_call x0 -> x1, Pallas kernels: none -> 76.1 us  [per_device(): pl.pallas_call(kernel, out_shape=jax.ShapeDtypeStruct((BANDL, OWN, CH), B...]
    dot_general x1 -> x0, matrix products: 18.2 us -> none  [cross_tile(): jnp.einsum('clm,dlm->lcd', weighted, coeffs, preferred_element_type=jnp.f...]
  transfers between devices with their start and end apart: 1 -> 0, of which waited for: 1 -> 0; matrix products, arithmetic and copies ran while one was open for 0% -> 0% of each run, Pallas kernels for 0% -> 0%
where the time goes in v1:
time: 79.4 us; the launch traced here: 79.3 us
  Pallas kernels  76.1 us (96%)
  local copies, waits for them, and re-layouts  3.13 us (4%)
    pallas_call x1, Pallas kernels, per_device(): pl.pallas_call(kernel, out_shape=jax.ShapeDtypeStruct((BANDL, OWN, CH), B...  76.1 us
    unnamed x5, local copies, waits for them, and re-layouts  3.13 us

profile of v1, /device:TPU:1, one launch (start us, length us, event | category | flops | bytes accessed | tf_op | source)
XLA Modules:
  0.0 79.3 jit_solution(12615085148589802069)
XLA Ops:
  0.0 0.0 copy-start
  0.0 1.3 %copy-done = bf16[32,16,1152]{2,1,0:T(8,128)(2,1)S(1)} copy-done((bf16[32,16,1152]{2,1,0:T(8,128)(2,1)S(1)}, bf16[32,16,1152]{2,1,0:T(8,128)(2,1)}, u32[]{:S(2)}) %copy-start) | copy-done | bytes 1179672
  1.3 0.0 copy-start.1
  1.3 0.9 %copy-done.1 = f32[16,1152]{1,0:T(8,128)S(1)} copy-done((f32[16,1152]{1,0:T(8,128)S(1)}, f32[16,1152]{1,0:T(8,128)}, u32[]{:S(2)}) %copy-start.1) | copy-done | bytes 73752
  2.2 76.1 %cross.1 = bf16[16,32,1024]{2,1,0:T(8,128)(2,1)S(1)} custom-call(bf16[32,16,1152]{2,1,0:T(8,128)(2,1)S(1)} %copy-done, f32[16,1152]{1,0:T(8,128)S(1)} %copy-done.1), custom_call_target="tpu_custom_call" | custom-call | flops 1207959552 | bytes 4194304 | tf_op jit(solution)/shard_map/cross/pallas_call | solution.py:172
  78.3 1.0 %copy.4 = bf16[16,32,1024]{2,1,0:T(8,128)(2,1)} copy(bf16[16,32,1024]{2,1,0:T(8,128)(2,1)S(1)} %cross.1) | data formatting | bytes 2097152
Async XLA Ops:
  0.0 1.3 %copy-start = (bf16[32,16,1152]{2,1,0:T(8,128)(2,1)S(1)}, bf16[32,16,1152]{2,1,0:T(8,128)(2,1)}, u32[]{:S(2)}) copy-start(bf16[32,16,1152]{2,1,0:T(8,128)(2,1)} %x_ref.1) | copy-start | bytes 3538948
  1.3 0.9 %copy-start.1 = (f32[16,1152]{1,0:T(8,128)S(1)}, f32[16,1152]{1,0:T(8,128)}, u32[]{:S(2)}) copy-start(f32[16,1152]{1,0:T(8,128)} %w_ref.1) | copy-start | bytes 221188

commit v2 on v1

--- a/solution.py
+++ b/solution.py
@@ -19,9 +19,9 @@
 
 
 def step_of(t):
-    u, dc = t // 2, t % 2
+    u, dx = t // 2, t % 2
     mag = 4 - (u + 1) // 2
-    return jnp.where(u % 2 == 1, mag, 8 - mag) % 8, dc
+    return jnp.where(u % 2 == 1, mag, 8 - mag) % 8, dx
 
 
 def kernel(
@@ -29,26 +29,26 @@
 ):
     k = lax.axis_index("chan")
     core, xh, z = k % 2, (k // 2) % 2, k // 4
-    me = 2 * z + core
+    me = 2 * z + xh
 
     def chan(zz, xx, cc):
         return (zz * 2 + xx) * 2 + cc
 
     def to(t):
-        dz, dc = step_of(t)
-        return (z + dz) % 8, (core + dc) % 2
+        dz, dx = step_of(t)
+        return (z + dz) % 8, (xh + dx) % 2
 
     def source(t):
-        dz, dc = step_of(t)
-        return (z + 8 - dz) % 8, (core + dc) % 2
+        dz, dx = step_of(t)
+        return (z + 8 - dz) % 8, (xh + dx) % 2
 
-    partner = chan(z, 1 - xh, core)
+    partner = chan(z, xh, 1 - core)
     barrier = pltpu.get_barrier_semaphore()
 
     def greet(t, carry):
-        zz, cc = source(t)
+        zz, xx = source(t)
         pl.semaphore_signal(
-            barrier, inc=1, device_id={"chan": chan(zz, xh, cc)}, device_id_type=MESH
+            barrier, inc=1, device_id={"chan": chan(zz, xx, core)}, device_id_type=MESH
         )
         return carry
 
@@ -66,19 +66,19 @@
         return pl.ds(pl.multiple_of(kk * OWN, OWN), OWN)
 
     def first(t):
-        zz, cc = to(t)
+        zz, xx = to(t)
         return pltpu.make_async_remote_copy(
-            src_ref=send.at[2 * zz + cc],
+            src_ref=send.at[2 * zz + xx],
             dst_ref=full.at[rows(k)],
             send_sem=s1.at[t],
             recv_sem=r1.at[t],
-            device_id={"chan": chan(zz, xh, cc)},
+            device_id={"chan": chan(zz, xx, core)},
             device_id_type=MESH,
         )
 
     def across(t):
-        zz, cc = source(t)
-        block = full.at[rows(chan(zz, xh, cc))]
+        zz, xx = source(t)
+        block = full.at[rows(chan(zz, xx, core))]
         return pltpu.make_async_remote_copy(
             src_ref=block,
             dst_ref=block,
@@ -115,20 +115,20 @@
     lax.fori_loop(0, 16, arrived, 0)
 
     def back(t):
-        zz, cc = to(t)
+        zz, xx = to(t)
         return pltpu.make_async_remote_copy(
             src_ref=stage.at[t],
             dst_ref=o_ref.at[me],
             send_sem=s3.at[t],
             recv_sem=r3.at[t],
-            device_id={"chan": chan(zz, xh, cc)},
+            device_id={"chan": chan(zz, xx, core)},
             device_id_type=MESH,
         )
 
     def chunk(u, last):
         for a in range(4):
-            zz, cc = to(4 * u + a)
-            block = full[rows(chan(zz, xh, cc)), :].astype(F32)
+            zz, xx = to(4 * u + a)
+            block = full[rows(chan(zz, xx, core)), :].astype(F32)
             left[pl.ds(a * OWN, OWN), :] = (block * scaled).astype(BF16)
         for n in range(CH // 256):
             tile = lax.dot_general(

time: 79.4 us -> 72.1 us (0.908)
  Pallas kernels: 76.1 us -> 68.8 us
    pallas_call x1, Pallas kernels: 76.1 us -> 68.8 us  [per_device(): pl.pallas_call(kernel, out_shape=jax.ShapeDtypeStruct((BANDL, OWN, CH), B...]
where the time goes in v2:
time: 72.1 us; the launch traced here: 71.9 us
  Pallas kernels  68.8 us (95%)
  local copies, waits for them, and re-layouts  3.13 us (4%)
    pallas_call x1, Pallas kernels, per_device(): pl.pallas_call(kernel, out_shape=jax.ShapeDtypeStruct((BANDL, OWN, CH), B...  68.8 us
    unnamed x5, local copies, waits for them, and re-layouts  3.13 us

profile of v2, /device:TPU:1, one launch (start us, length us, event | category | flops | bytes accessed | tf_op | source)
XLA Modules:
  0.0 71.9 jit_solution(4024210076633125048)
XLA Ops:
  0.0 0.0 copy-start
  0.0 1.3 %copy-done = bf16[32,16,1152]{2,1,0:T(8,128)(2,1)S(1)} copy-done((bf16[32,16,1152]{2,1,0:T(8,128)(2,1)S(1)}, bf16[32,16,1152]{2,1,0:T(8,128)(2,1)}, u32[]{:S(2)}) %copy-start) | copy-done | bytes 1179672
  1.3 0.0 copy-start.1
  1.3 0.9 %copy-done.1 = f32[16,1152]{1,0:T(8,128)S(1)} copy-done((f32[16,1152]{1,0:T(8,128)S(1)}, f32[16,1152]{1,0:T(8,128)}, u32[]{:S(2)}) %copy-start.1) | copy-done | bytes 73752
  2.2 68.8 %cross.1 = bf16[16,32,1024]{2,1,0:T(8,128)(2,1)S(1)} custom-call(bf16[32,16,1152]{2,1,0:T(8,128)(2,1)S(1)} %copy-done, f32[16,1152]{1,0:T(8,128)S(1)} %copy-done.1), custom_call_target="tpu_custom_call" | custom-call | flops 1207959552 | bytes 4194304 | tf_op jit(solution)/shard_map/cross/pallas_call | solution.py:172
  70.9 1.0 %copy.4 = bf16[16,32,1024]{2,1,0:T(8,128)(2,1)} copy(bf16[16,32,1024]{2,1,0:T(8,128)(2,1)S(1)} %cross.1) | data formatting | bytes 2097152
Async XLA Ops:
  0.0 1.3 %copy-start = (bf16[32,16,1152]{2,1,0:T(8,128)(2,1)S(1)}, bf16[32,16,1152]{2,1,0:T(8,128)(2,1)}, u32[]{:S(2)}) copy-start(bf16[32,16,1152]{2,1,0:T(8,128)(2,1)} %x_ref.1) | copy-start | bytes 3538948
  1.3 0.9 %copy-start.1 = (f32[16,1152]{1,0:T(8,128)S(1)}, f32[16,1152]{1,0:T(8,128)}, u32[]{:S(2)}) copy-start(f32[16,1152]{1,0:T(8,128)} %w_ref.1) | copy-start | bytes 221188

commit v3 on v0

v3 whole, which is shorter than its diff:
```python
import jax
import jax.numpy as jnp
from jax import lax
from jax.experimental import pallas as pl
from jax.experimental.pallas import tpu as pltpu
from jax.sharding import PartitionSpec as P

MESH = pl.DeviceIdType.MESH
BF16 = jnp.bfloat16
F32 = jnp.float32

ZS = 8
OWN = 32
BANDL = 16
ML = 1152
CH = 1024


def kernel(
    x_hbm, w_hbm, o_ref, x_ref, w_ref, send, own, zb, wown, wz, stage,
    in_sem, x_send, x_recv, c_send, co_recv, cz_recv, z_send, z_recv, o_send, o_recv,
):
    loads = [
        pltpu.make_async_copy(x_hbm, x_ref, in_sem.at[0]),
        pltpu.make_async_copy(w_hbm, w_ref, in_sem.at[1]),
    ]
    for load in loads:
        load.start()
    dev = lax.axis_index("chan")
    core, xh, z = dev % 2, (dev // 2) % 2, dev // 4

    def chan(zz, xx, cc):
        return {"chan": ((zz % ZS) * 2 + xx) * 2 + cc}

    def up(way, k):
        return (z + ZS + jnp.where(way == 0, k, -k)) % ZS

    barrier = pltpu.get_barrier_semaphore()

    def greet(t, carry):
        pl.semaphore_signal(
            barrier, inc=1, device_id=chan(z + t // 2, (xh + t) % 2, core), device_id_type=MESH
        )
        return carry

    lax.fori_loop(1, 16, greet, 0)
    pl.semaphore_signal(barrier, inc=1, device_id=chan(z, xh, 1 - core), device_id_type=MESH)

    def part(cc, hh):
        return pl.ds(pl.multiple_of((cc * 2 + hh) * OWN, OWN), OWN)

    def remote(src, dst, s, r, to):
        return pltpu.make_async_remote_copy(
            src_ref=src, dst_ref=dst, send_sem=s, recv_sem=r, device_id=to, device_id_type=MESH
        )

    def active(way, k, j):
        return jnp.logical_or(j + k < 4, (z + k + way) % 2 == 0)

    loads[0].wait()
    for c in range(ML // 128):
        cols = pl.ds(c * 128, 128)
        send[:, :, cols] = jnp.swapaxes(x_ref[:, :, cols], 0, 1)
    pl.semaphore_wait(barrier, 16)

    def z_own(way, k, hh, src):
        remote(
            src, zb.at[way, k - 1, 0, part(core, hh)], z_send, z_recv.at[way, k - 1, 0, hh],
            chan(up(way, 1), xh, core),
        ).start()

    def x_copy(p):
        return remote(
            send.at[2 * p + 1 - xh], own.at[p, part(core, xh)], x_send, x_recv.at[p],
            chan(z, 1 - xh, core),
        )

    def x_wait(p):
        block = own.at[p, part(core, 1 - xh)]
        remote(block, block, x_send, x_recv.at[p], chan(z, 1 - xh, core)).wait_recv()

    def c_own(p, hh, src):
        remote(
            src, own.at[p, part(core, hh)], c_send, co_recv.at[p, hh], chan(z, xh, 1 - core)
        ).start()

    def out(k):
        for way in range(2):
            p = up(way, k)
            src = send.at[2 * p + xh]
            if k == 4:
                pl.when(active(way, 4, 0))(lambda: z_own(way, 4, xh, src))
                if way == 0:
                    x_copy(p).start()
            else:
                z_own(way, k, xh, src)
                x_copy(p).start()

    for k in (4, 3, 2, 1):
        out(k)
    x_copy(z).start()

    def keep(p, carry):
        block = send.at[2 * p + xh]
        c_own(p, xh, block)
        own[p, part(core, xh), :] = block[...]
        return carry

    lax.fori_loop(0, ZS, keep, 0)

    def take_x(way, k):
        p = up(way, k)
        x_wait(p)
        src = own.at[p, part(core, 1 - xh)]
        if k == 4:
            for w in range(2):
                pl.when(active(w, 4, 0))(lambda: z_own(w, 4, 1 - xh, src))
        elif k > 0:
            z_own(way, k, 1 - xh, src)
        c_own(p, 1 - xh, src)

    def take_z(way, k, j, hh):
        def go():
            block = zb.at[way, k, j - 1, part(core, hh)]
            remote(
                block, block, z_send, z_recv.at[way, k, j - 1, hh], chan(z, xh, core)
            ).wait_recv()
            if k > 0:
                remote(
                    block, zb.at[way, k - 1, j, part(core, hh)], z_send,
                    z_recv.at[way, k - 1, j, hh], chan(up(way, 1), xh, core),
                ).start()
            remote(
                block, block, c_send, cz_recv.at[way, k, j - 1, hh], chan(z, xh, 1 - core)
            ).start()

        if j + k == 4:
            pl.when(active(way, k, j))(go)
        else:
            go()

    def both(k, j, hh):
        take_z(0, k, j, hh)
        take_z(1, k, j, hh)

    def scaled(p):
        return w_ref[pl.ds(2 * p + xh, 1), :]

    def mine():
        return pl.ds(pl.multiple_of(core * 2 * OWN, 2 * OWN), 2 * OWN)

    def natural(ref):
        return jnp.concatenate([ref[i * OWN : (i + 1) * OWN, :] for i in (0, 2, 1, 3)], axis=0)

    def dot(left, right):
        return lax.dot_general(
            left, right, (((1,), (1,)), ((), ())), preferred_element_type=F32
        ).astype(BF16)

    def emit(slot, value, p, row_z, col_z, home):
        stage[slot, 0] = value[:OWN]
        stage[slot, 1] = value[OWN:]
        place = o_ref.at[2 * p + xh, :, pl.ds(pl.multiple_of(col_z * 128, 128), 128)]
        if home:
            pltpu.make_async_copy(stage.at[slot, xh], place, o_recv).start()
            halves = (1 - xh,)
        else:
            halves = (0, 1)
        for hh in halves:
            remote(stage.at[slot, hh], place, o_send, o_recv, chan(row_z, hh, core)).start()

    def weigh(block, p):
        return (block.astype(F32) * scaled(p)).astype(BF16)

    def pair(way, k, j):
        p, far = up(way, k), up(way, -j)
        for hh in range(2):
            block = zb.at[way, k, j - 1, part(1 - core, hh)]
            remote(
                block, block, c_send, cz_recv.at[way, k, j - 1, hh], chan(z, xh, 1 - core)
            ).wait_recv()
        block = zb.at[way, k, j - 1]
        slot = 2 * ((way * 4 + k) * 4 + j - 1)
        theirs = weigh(zb[way, k, j - 1, mine(), :], p)

        @pl.when(k == 0)
        def _():
            wz[way, j - 1] = theirs

        emit(slot, dot(theirs, natural(own.at[p])), p, far, z, False)
        emit(slot + 1, dot(wown[p], natural(block)), p, z, far, True)

    def pairs(j):
        def step(t, carry):
            way, k = t % 2, (4 - j) - t // 2
            pl.when(active(way, k, j))(lambda: pair(way, k, j))
            return carry

        lax.fori_loop(0, 2 * (5 - j), step, 0)

    def cross(way, ja, jb):
        value = dot(wz[way, ja - 1], natural(zb.at[1 - way, 0, jb - 1]))
        slot = 72 + (way * 4 + ja - 1) * 4 + jb - 1
        emit(slot, value, z, up(way, -ja), up(way, jb), False)

    def crosses(j):
        def step(t, carry):
            way, i = t % 2, t // 2
            far = i < j
            cross(way, jnp.where(far, j, i - j + 1), jnp.where(far, i + 1, j))
            return carry

        lax.fori_loop(0, 2 * (2 * j - 1), step, 0)

    def crosses_last():
        way = z % 2

        def step(t, carry):
            i = t // 2
            far = t % 2 == 0
            cross(
                jnp.where(far, way, 1 - way), jnp.where(far, 4, i + 1), jnp.where(far, i + 1, 4)
            )
            return carry

        lax.fori_loop(0, 6, step, 0)

    def diagonal(p, carry):
        for hh in range(2):
            block = own.at[p, part(1 - core, hh)]
            remote(
                block, block, c_send, co_recv.at[p, hh], chan(z, xh, 1 - core)
            ).wait_recv()
        left = weigh(own[p, mine(), :], p)
        wown[p] = left
        emit(64 + p, dot(left, natural(own.at[p])), p, z, z, True)
        return carry

    take_x(0, 4)
    both(3, 1, xh)
    take_x(0, 3)
    both(2, 1, xh)
    take_x(1, 3)
    both(1, 1, xh)
    take_x(0, 2)
    both(0, 1, xh)
    take_x(1, 2)
    both(3, 1, 1 - xh)
    take_x(0, 1)
    both(2, 1, 1 - xh)
    take_x(1, 1)
    both(1, 1, 1 - xh)
    take_x(0, 0)
    loads[1].wait()
    weights = w_ref[...]
    w_ref[...] = weights / jnp.sum(weights, axis=1, keepdims=True)
    lax.fori_loop(0, ZS, diagonal, 0)
    both(0, 1, 1 - xh)
    pairs(1)
    for j in (2, 3, 4):
        for hh in (xh, 1 - xh):
            for k in range(4 - j, -1, -1):
                both(k, j, hh)
        crosses(j - 1)
        pairs(j)
    crosses_last()

    def drain(ref, sem):
        pltpu.make_async_copy(ref, ref, sem).wait()

    drain(o_ref, o_recv)
    drain(stage.at[pl.ds(0, 52)], o_send)
    drain(own, z_send)
    drain(zb.at[0, pl.ds(0, 3)], c_send)
    drain(send.at[pl.ds(0, 8)], x_send)


def per_device(spectra, weights):
    dma = pltpu.SemaphoreType.DMA
    return pl.pallas_call(
        kernel,
        out_shape=jax.ShapeDtypeStruct((BANDL, OWN, CH), BF16),
        in_specs=[pl.BlockSpec(memory_space=pl.ANY)] * 2,
        out_specs=pl.BlockSpec(memory_space=pl.ANY),
        scratch_shapes=[
            pltpu.VMEM((OWN, BANDL, ML), BF16),
            pltpu.VMEM((BANDL, ML), F32),
            pltpu.VMEM((BANDL, OWN, ML), BF16),
            pltpu.VMEM((ZS, 4 * OWN, ML), BF16),
            pltpu.VMEM((2, 4, 4, 4 * OWN, ML), BF16),
            pltpu.VMEM((ZS, 2 * OWN, ML), BF16),
            pltpu.VMEM((2, 4, 2 * OWN, ML), BF16),
            pltpu.VMEM((104, 2, OWN, 128), BF16),
            dma((2,)),
            dma,
            dma((ZS,)),
            dma,
            dma((ZS, 2)),
            dma((2, 4, 4, 2)),
            dma,
            dma((2, 4, 4, 2)),
            dma,
            dma,
        ],
        compiler_params=pltpu.CompilerParams(
            collective_id=0, has_side_effects=True, vmem_limit_bytes=60 << 20
        ),
        cost_estimate=pl.CostEstimate(
            flops=2 * BANDL * OWN * CH * ML, bytes_accessed=4 << 20, transcendentals=0
        ),
        name="cross",
    )(spectra, weights)


def solution(mesh):
    placed = (P("chan", "band", None), P("band", None))
    return jax.shard_map(
        per_device, mesh=mesh, in_specs=placed, out_specs=P("band", "chan", None), check_vma=False
    )
```

time: 291 us -> 62.4 us (0.21)
  waiting for transfers between devices: 255 us -> 0 us
  Pallas kernels: 0 us -> 59.9 us
  matrix products: 18.2 us -> 0 us
  between operations: 13.4 us -> 0.01 us
    all_gather x1 -> x0, waiting for transfers between devices: 255 us -> none  [per_device(): lax.all_gather(spectra, 'chan', axis=0, tiled=True)]
    pallas_call x0 -> x1, Pallas kernels: none -> 59.9 us  [per_device(): pl.pallas_call(kernel, out_shape=jax.ShapeDtypeStruct((BANDL, OWN, CH), B...]
    dot_general x1 -> x0, matrix products: 18.2 us -> none  [cross_tile(): jnp.einsum('clm,dlm->lcd', weighted, coeffs, preferred_element_type=jnp.f...]
  transfers between devices with their start and end apart: 1 -> 0, of which waited for: 1 -> 0; matrix products, arithmetic and copies ran while one was open for 0% -> 0% of each run, Pallas kernels for 0% -> 0%
where the time goes in v3:
time: 62.4 us; the launch traced here: 62.2 us
  Pallas kernels  59.9 us (96%)
  local copies, waits for them, and re-layouts  2.29 us (4%)
    pallas_call x1, Pallas kernels, per_device(): pl.pallas_call(kernel, out_shape=jax.ShapeDtypeStruct((BANDL, OWN, CH), B...  59.9 us
    unnamed x1, local copies, waits for them, and re-layouts  2.29 us

profile of v3, /device:TPU:1, one launch (start us, length us, event | category | flops | bytes accessed | tf_op | source)
XLA Modules:
  0.0 62.2 jit_solution(1045076931436681089)
XLA Ops:
  0.0 59.9 %cross.1 = bf16[16,32,1024]{2,1,0:T(8,128)(2,1)} custom-call(bf16[32,16,1152]{2,1,0:T(8,128)(2,1)} %x_hbm.1, f32[16,1152]{1,0:T(8,128)} %w_hbm.1), custom_call_target="tpu_custom_call" | custom-call | flops 1207959552 | bytes 4194304 | tf_op jit(solution)/shard_map/cross/pallas_call | solution.py:280
  59.9 2.3 %copy.4 = bf16[16,32,1024]{2,1,0:T(8,128)(2,1)} copy(bf16[16,32,1024]{2,1,0:T(8,128)(2,1)} %cross.1) | data formatting | bytes 2097152

commit v4 on v0

v4 whole, which is shorter than its diff:
```python
import jax
import jax.numpy as jnp
from jax import lax
from jax.experimental import pallas as pl
from jax.experimental.pallas import tpu as pltpu
from jax.sharding import PartitionSpec as P

MESH = pl.DeviceIdType.MESH
BF16 = jnp.bfloat16
F32 = jnp.float32

ZS = 8
OWN = 32
PER = 128
BANDL = 16
ML = 1152
CH = 1024

ORDER = (((0, 4), (0, 2), (1, 2), (0, 0)), ((0, 3), (1, 3), (0, 1), (1, 1)))


PLAN = (
    (
        ('F', 0, 4),
        ('F', 1, 2),
        ('F', 0, 2),
        ('F', 0, 0),
        ('O', 0, 4),
        ('T', 1, 2, 1, 0),
        ('T', 0, 2, 1, 0),
        ('O', 0, 2),
        ('O', 1, 2),
        ('T', 1, 2, 1, 1),
        ('T', 0, 2, 1, 1),
        ('B', 0, 2, 1),
        ('B', 1, 2, 1),
        ('O', 0, 0),
        ('T', 0, 2, 2, 0),
        ('T', 0, 2, 2, 1),
        ('T', 0, 0, 1, 0),
        ('T', 0, 0, 1, 1),
        ('T', 1, 0, 1, 0),
        ('T', 1, 0, 1, 1),
        ('W', 0, 7, 1),
        ('X', 7, 1, 0, 2),
        ('X', 1, 1, 0, 1),
        ('B', 0, 2, 2),
        ('T', 0, 0, 2, 0),
        ('T', 0, 0, 2, 1),
        ('T', 1, 0, 2, 0),
        ('T', 1, 0, 2, 1),
        ('W', 6, 2),
        ('X', 6, 1, 0, 3),
        ('X', 2, 1, 0, 1),
        ('X', 1, 2, 6, 2),
        ('T', 0, 0, 3, 0),
        ('T', 0, 0, 3, 1),
        ('T', 1, 0, 3, 0),
        ('T', 1, 0, 3, 1),
        ('W', 5, 3),
        ('X', 5, 1, 0, 4),
        ('X', 7, 1, 2, 2),
        ('X', 3, 1, 6, 2),
        ('X', 6, 1, 3, 1),
        ('X', 3, 1, 0, 1),
        ('H', 0, 4, 4, 1),
        ('H', 0, 2, 4, 3),
        ('H', 1, 2, 2, 2),
        ('T', 0, 0, 4, 0),
        ('T', 0, 0, 4, 1),
        ('W', 4),
        ('X', 4, 1, 0, 4),
        ('X', 1, 3, 4, 2),
        ('H', 0, 0, 0, 4),
        ('H', 0, 0, 4, 4),
    ),
    (
        ('F', 0, 3),
        ('F', 1, 3),
        ('O', 0, 3),
        ('T', 0, 3, 1, 0),
        ('F', 0, 1),
        ('F', 1, 1),
        ('O', 1, 3),
        ('T', 0, 3, 1, 1),
        ('T', 0, 1, 1, 0),
        ('T', 1, 1, 1, 0),
        ('T', 0, 1, 1, 1),
        ('T', 1, 1, 1, 1),
        ('O', 0, 1),
        ('O', 1, 1),
        ('B', 0, 1, 1),
        ('B', 1, 1, 1),
        ('B', 0, 3, 1),
        ('T', 0, 1, 2, 0),
        ('T', 1, 1, 2, 0),
        ('T', 0, 1, 2, 1),
        ('T', 1, 1, 2, 1),
        ('B', 0, 1, 2),
        ('B', 1, 1, 2),
        ('T', 0, 1, 3, 0),
        ('T', 0, 1, 3, 1),
        ('B', 0, 1, 3),
        ('H', 1, 3, 3, 1),
        ('H', 0, 3, 4, 2),
        ('H', 1, 1, 1, 3),
        ('H', 0, 1, 4, 4),
    ),
)


def place(way, k):
    return k if way else (ZS - k) % ZS


def kernel(
    x_hbm, w_hbm, o_ref, x_ref, w_ref, send, ring, weighted, stage, found,
    in_sem, l_send, l_recv, z_send, z_recv, o_send, o_recv,
):
    loads = [
        pltpu.make_async_copy(x_hbm, x_ref, in_sem.at[0]),
        pltpu.make_async_copy(w_hbm, w_ref, in_sem.at[1]),
    ]
    for load in loads:
        load.start()
    dev = lax.axis_index("chan")
    core, xh, z = dev % 2, (dev // 2) % 2, dev // 4

    def chan(zz, xx, cc):
        return {"chan": ((zz % ZS) * 2 + xx) * 2 + cc}

    barrier = pltpu.get_barrier_semaphore()
    for there in (
        chan(z + 1, xh, core), chan(z + ZS - 1, xh, core),
        chan(z, xh, 1 - core), chan(z, 1 - xh, 0), chan(z, 1 - xh, 1),
    ):
        pl.semaphore_signal(barrier, inc=1, device_id=there, device_id_type=MESH)

    def part(hh, cc):
        return pl.ds(pl.multiple_of((hh * 2 + cc) * OWN, OWN), OWN)

    def half(hh):
        return pl.ds(pl.multiple_of(hh * 2 * OWN, 2 * OWN), 2 * OWN)

    def remote(src, dst, s, r, to):
        return pltpu.make_async_remote_copy(
            src_ref=src, dst_ref=dst, send_sem=s, recv_sem=r, device_id=to, device_id_type=MESH
        )

    def up(way, k, cc=None):
        cc = core if cc is None else cc
        return (z + ZS + jnp.where((cc + way) % 2 == 0, k, -k)) % ZS

    loads[0].wait()
    for c in range(ML // 128):
        cols = pl.ds(c * 128, 128)
        send[:, :, cols] = jnp.swapaxes(x_ref[:, :, cols], 0, 1)
    pl.semaphore_wait(barrier, 5)

    def give(p, there, hh, cc):
        q = p // 2
        remote(
            send.at[2 * p + hh], ring.at[q * ZS + there, part(xh, core)], l_send,
            l_recv.at[q, xh * 2 + core], chan(z, hh, cc),
        ).start()

    def got(way, k, hh, cc):
        q = up(way, k) // 2
        block = ring.at[q * ZS + place(way, k), part(hh, cc)]
        remote(block, block, l_send, l_recv.at[q, hh * 2 + cc], chan(z, 1 - xh, core)).wait_recv()

    def z_copy(way, k, j, hh):
        at = (up(way, k) // 2) * ZS + place(way, k + j)
        block = ring.at[at, half(hh)]
        return remote(block, block, z_send, z_recv.at[at, hh], chan(up(way, 1), xh, core))

    def take(way, k, j, hh):
        copy = z_copy(way, k, j, hh)
        copy.wait_recv()
        if k > 0:
            copy.start()

    def take_all(*which):
        for hh in (xh, 1 - xh):
            for way, k, j in which:
                take(way, k, j, hh)

    def rows_of(way, k, lo, n):
        return ring[pl.ds((up(way, k) // 2) * ZS + lo, n)].reshape(n * PER, ML)

    def dot(left, right):
        return lax.dot_general(
            left, right, (((1,), (1,)), ((), ())), preferred_element_type=F32
        ).astype(BF16)

    def weigh(block, p):
        return (block.astype(F32) * w_ref[pl.ds(2 * p + xh, 1), :]).astype(BF16)

    slots = [0]

    def emit(value, p, row_z, lo, n, home=False):
        slot = slots[0]
        slots[0] += 4
        cols = pl.ds(lo * PER, n * PER)
        for i in range(4):
            stage[slot + i, :, 0 : n * PER] = value[i * OWN : (i + 1) * OWN]
        if home:
            found[2 * p + xh, :, cols] = stage[slot + 2 * xh + core, :, 0 : n * PER]
            others = ((xh, 1 - core), (1 - xh, 0), (1 - xh, 1))
        else:
            others = ((0, 0), (0, 1), (1, 0), (1, 1))
        for hh, cc in others:
            remote(
                stage.at[slot + 2 * hh + cc, :, pl.ds(0, n * PER)], found.at[2 * p + xh, :, cols],
                o_send, o_recv, chan(row_z, hh, cc),
            ).start()

    def home(way, k, lo, n):
        p = up(way, k)
        left = weigh(rows_of(way, k, place(way, k), 1), p)
        emit(dot(left, rows_of(way, k, lo, n)), p, z, lo, n, home=True)

    def behind(way, k, j):
        p = up(way, k)
        left = weigh(rows_of(way, k, place(way, k + j), 1), p)
        emit(dot(left, rows_of(way, k, place(way, k), 1)), p, up(way, -j), place(way, k), 1)

    def weigh_all(*places):
        for at in places:
            weighted[at] = weigh(rows_of(0, 0, at, 1), z)

    def across(first, count, lo, n):
        left = weighted[pl.ds(first, count)].reshape(count * PER, ML)
        value = dot(left, rows_of(0, 0, lo, n))
        for i in range(count):
            emit(value[i * PER : (i + 1) * PER], z, up(0, first + i), lo, n)

    def run(e):
        slots[0] = 0
        mine, other = ORDER[e], ORDER[1 - e]
        for (way, k), (oway, ok) in zip(mine, other):
            p, op = up(way, k), up(oway, ok, 1 - core)
            give(op, place(oway, ok), xh, 1 - core)
            give(p, place(way, k), 1 - xh, core)
            give(op, place(oway, ok), 1 - xh, 1 - core)
        for way, k in mine:
            p = up(way, k)
            ring[(p // 2) * ZS + place(way, k), part(xh, core), :] = send[2 * p + xh]
        loads[1].wait()
        weights = w_ref[...]
        w_ref[...] = weights / jnp.sum(weights, axis=1, keepdims=True)

        def side(h):
            return xh if h == 0 else 1 - xh

        def first_half(way, k):
            got(way, k, xh, 1 - core)
            if k > 0:
                z_copy(way, k, 0, xh).start()

        def other_half(way, k):
            got(way, k, 1 - xh, 0)
            got(way, k, 1 - xh, 1)
            if k > 0:
                z_copy(way, k, 0, 1 - xh).start()

        def takes(way, k, j, h):
            take(way, k, j, side(h))

        todo = {
            "F": first_half,
            "O": other_half,
            "T": takes,
            "B": behind,
            "H": home,
            "W": weigh_all,
            "X": across,
        }
        for what, *numbers in PLAN[e]:
            todo[what](*numbers)

        def drain(ref, sem):
            pltpu.make_async_copy(ref, ref, sem).wait()

        drain(stage.at[pl.ds(0, 57 if e == 0 else 59), :, pl.ds(0, 2 * PER)], o_recv)
        for p in range(ZS):
            for place_z in range(ZS):
                at = (place_z - p if p % 2 == 0 else p - place_z) % ZS
                o_ref[2 * p : 2 * p + 2, :, place_z * PER : (place_z + 1) * PER] = found[
                    2 * p : 2 * p + 2, :, at * PER : (at + 1) * PER
                ]
        drain(stage.at[pl.ds(0, 89 if e == 0 else 27), :, pl.ds(0, 2 * PER)], o_send)
        drain(ring.at[pl.ds(0, 6 if e == 0 else 10)], z_send)
        drain(send.at[pl.ds(0, 12)], l_send)

    pl.when((z + core) % 2 == 0)(lambda: run(0))
    pl.when((z + core) % 2 == 1)(lambda: run(1))


def per_device(spectra, weights):
    dma = pltpu.SemaphoreType.DMA
    return pl.pallas_call(
        kernel,
        out_shape=jax.ShapeDtypeStruct((BANDL, OWN, CH), BF16),
        in_specs=[pl.BlockSpec(memory_space=pl.ANY)] * 2,
        out_specs=pl.BlockSpec(memory_space=pltpu.VMEM),
        scratch_shapes=[
            pltpu.VMEM((OWN, BANDL, ML), BF16),
            pltpu.VMEM((BANDL, ML), F32),
            pltpu.VMEM((BANDL, OWN, ML), BF16),
            pltpu.VMEM((4 * ZS, PER, ML), BF16),
            pltpu.VMEM((ZS, PER, ML), BF16),
            pltpu.VMEM((108, OWN, 4 * PER), BF16),
            pltpu.VMEM((BANDL, OWN, CH), BF16),
            dma((2,)),
            dma,
            dma((4, 4)),
            dma,
            dma((4 * ZS, 2)),
            dma,
            dma,
        ],
        compiler_params=pltpu.CompilerParams(
            collective_id=0, has_side_effects=True, vmem_limit_bytes=54000 << 10
        ),
        cost_estimate=pl.CostEstimate(
            flops=2 * BANDL * OWN * CH * ML, bytes_accessed=4 << 20, transcendentals=0
        ),
        name="cross",
    )(spectra, weights)


def solution(mesh):
    placed = (P("chan", "band", None), P("band", None))
    return jax.shard_map(
        per_device, mesh=mesh, in_specs=placed, out_specs=P("band", "chan", None), check_vma=False
    )
```

time: 291 us -> 58.6 us (0.20)
  waiting for transfers between devices: 255 us -> 0 us
  Pallas kernels: 0 us -> 56.6 us
  matrix products: 18.2 us -> 0 us
  between operations: 13.4 us -> 0.01 us
    all_gather x1 -> x0, waiting for transfers between devices: 255 us -> none  [per_device(): lax.all_gather(spectra, 'chan', axis=0, tiled=True)]
    pallas_call x0 -> x1, Pallas kernels: none -> 56.6 us  [per_device(): pl.pallas_call(kernel, out_shape=jax.ShapeDtypeStruct((BANDL, OWN, CH), B...]
    dot_general x1 -> x0, matrix products: 18.2 us -> none  [cross_tile(): jnp.einsum('clm,dlm->lcd', weighted, coeffs, preferred_element_type=jnp.f...]
  transfers between devices with their start and end apart: 1 -> 0, of which waited for: 1 -> 0; matrix products, arithmetic and copies ran while one was open for 0% -> 0% of each run, Pallas kernels for 0% -> 0%
where the time goes in v4:
time: 58.6 us; the launch traced here: 58.5 us
  Pallas kernels  56.6 us (97%)
  local copies, waits for them, and re-layouts  1.86 us (3%)
    pallas_call x1, Pallas kernels, per_device(): pl.pallas_call(kernel, out_shape=jax.ShapeDtypeStruct((BANDL, OWN, CH), B...  56.6 us
    unnamed x3, local copies, waits for them, and re-layouts  1.86 us

profile of v4, /device:TPU:1, one launch (start us, length us, event | category | flops | bytes accessed | tf_op | source)
XLA Modules:
  0.0 58.5 jit_solution(3294377289634471257)
XLA Ops:
  0.0 0.0 copy-start
  0.0 0.9 %copy-done = f32[16,1152]{1,0:T(8,128)S(1)} copy-done((f32[16,1152]{1,0:T(8,128)S(1)}, f32[16,1152]{1,0:T(8,128)}, u32[]{:S(2)}) %copy-start) | copy-done | bytes 73752
  0.9 56.6 %cross.1 = bf16[16,32,1024]{2,1,0:T(8,128)(2,1)S(1)} custom-call(bf16[32,16,1152]{2,1,0:T(8,128)(2,1)} %x_hbm.1, f32[16,1152]{1,0:T(8,128)S(1)} %copy-done), custom_call_target="tpu_custom_call" | custom-call | flops 1207959552 | bytes 4194304 | tf_op jit(solution)/shard_map/cross/pallas_call | solution.py:302
  57.5 1.0 %copy.4 = bf16[16,32,1024]{2,1,0:T(8,128)(2,1)} copy(bf16[16,32,1024]{2,1,0:T(8,128)(2,1)S(1)} %cross.1) | data formatting | bytes 2097152
Async XLA Ops:
  0.0 0.9 %copy-start = (f32[16,1152]{1,0:T(8,128)S(1)}, f32[16,1152]{1,0:T(8,128)}, u32[]{:S(2)}) copy-start(f32[16,1152]{1,0:T(8,128)} %w_hbm.1) | copy-start | bytes 221188

commit v5 on v4

--- a/solution.py
+++ b/solution.py
@@ -77,29 +77,29 @@
     (
         ('F', 0, 3),
         ('F', 1, 3),
+        ('F', 0, 1),
         ('O', 0, 3),
         ('T', 0, 3, 1, 0),
-        ('F', 0, 1),
         ('F', 1, 1),
         ('O', 1, 3),
         ('T', 0, 3, 1, 1),
+        ('T', 1, 1, 1, 0),
         ('T', 0, 1, 1, 0),
-        ('T', 1, 1, 1, 0),
+        ('T', 1, 1, 1, 1),
         ('T', 0, 1, 1, 1),
-        ('T', 1, 1, 1, 1),
+        ('T', 1, 1, 2, 0),
+        ('O', 1, 1),
+        ('T', 0, 1, 2, 0),
         ('O', 0, 1),
-        ('O', 1, 1),
+        ('T', 1, 1, 2, 1),
+        ('T', 0, 1, 2, 1),
+        ('T', 0, 1, 3, 0),
+        ('T', 0, 1, 3, 1),
         ('B', 0, 1, 1),
         ('B', 1, 1, 1),
         ('B', 0, 3, 1),
-        ('T', 0, 1, 2, 0),
-        ('T', 1, 1, 2, 0),
-        ('T', 0, 1, 2, 1),
-        ('T', 1, 1, 2, 1),
         ('B', 0, 1, 2),
         ('B', 1, 1, 2),
-        ('T', 0, 1, 3, 0),
-        ('T', 0, 1, 3, 1),
         ('B', 0, 1, 3),
         ('H', 1, 3, 3, 1),
         ('H', 0, 3, 4, 2),

time: 58.6 us -> 56.8 us (0.969)
  Pallas kernels: 56.6 us -> 54.8 us
    pallas_call x1, Pallas kernels: 56.6 us -> 54.8 us  [per_device(): pl.pallas_call(kernel, out_shape=jax.ShapeDtypeStruct((BANDL, OWN, CH), B...]
where the time goes in v5:
time: 56.8 us; the launch traced here: 56.7 us
  Pallas kernels  54.8 us (96%)
  local copies, waits for them, and re-layouts  1.86 us (3%)
    pallas_call x1, Pallas kernels, per_device(): pl.pallas_call(kernel, out_shape=jax.ShapeDtypeStruct((BANDL, OWN, CH), B...  54.8 us
    unnamed x3, local copies, waits for them, and re-layouts  1.86 us

profile of v5, /device:TPU:1, one launch (start us, length us, event | category | flops | bytes accessed | tf_op | source)
XLA Modules:
  0.0 56.7 jit_solution(8729701924801828673)
XLA Ops:
  0.0 0.0 copy-start
  0.0 0.9 %copy-done = f32[16,1152]{1,0:T(8,128)S(1)} copy-done((f32[16,1152]{1,0:T(8,128)S(1)}, f32[16,1152]{1,0:T(8,128)}, u32[]{:S(2)}) %copy-start) | copy-done | bytes 73752
  0.9 54.8 %cross.1 = bf16[16,32,1024]{2,1,0:T(8,128)(2,1)S(1)} custom-call(bf16[32,16,1152]{2,1,0:T(8,128)(2,1)} %x_hbm.1, f32[16,1152]{1,0:T(8,128)S(1)} %copy-done), custom_call_target="tpu_custom_call" | custom-call | flops 1207959552 | bytes 4194304 | tf_op jit(solution)/shard_map/cross/pallas_call | solution.py:302
  55.7 1.0 %copy.4 = bf16[16,32,1024]{2,1,0:T(8,128)(2,1)} copy(bf16[16,32,1024]{2,1,0:T(8,128)(2,1)S(1)} %cross.1) | data formatting | bytes 2097152
Async XLA Ops:
  0.0 0.9 %copy-start = (f32[16,1152]{1,0:T(8,128)S(1)}, f32[16,1152]{1,0:T(8,128)}, u32[]{:S(2)}) copy-start(f32[16,1152]{1,0:T(8,128)} %w_hbm.1) | copy-start | bytes 221188

commit v6 on v5

--- a/solution.py
+++ b/solution.py
@@ -22,57 +22,57 @@
 PLAN = (
     (
         ('F', 0, 4),
+        ('F', 0, 2),
         ('F', 1, 2),
-        ('F', 0, 2),
         ('F', 0, 0),
         ('O', 0, 4),
+        ('T', 0, 2, 1, 0),
         ('T', 1, 2, 1, 0),
-        ('T', 0, 2, 1, 0),
         ('O', 0, 2),
         ('O', 1, 2),
+        ('T', 0, 2, 1, 1),
         ('T', 1, 2, 1, 1),
-        ('T', 0, 2, 1, 1),
-        ('B', 0, 2, 1),
-        ('B', 1, 2, 1),
         ('O', 0, 0),
         ('T', 0, 2, 2, 0),
         ('T', 0, 2, 2, 1),
+        ('B', 0, 2, 1),
+        ('B', 1, 2, 1),
+        ('B', 0, 2, 2),
         ('T', 0, 0, 1, 0),
         ('T', 0, 0, 1, 1),
         ('T', 1, 0, 1, 0),
         ('T', 1, 0, 1, 1),
-        ('W', 0, 7, 1),
-        ('X', 7, 1, 0, 2),
-        ('X', 1, 1, 0, 1),
-        ('B', 0, 2, 2),
+        ('W', 3, 4, 5),
+        ('X', 3, 1, 4, 2),
+        ('X', 5, 1, 3, 2),
         ('T', 0, 0, 2, 0),
         ('T', 0, 0, 2, 1),
         ('T', 1, 0, 2, 0),
         ('T', 1, 0, 2, 1),
-        ('W', 6, 2),
-        ('X', 6, 1, 0, 3),
-        ('X', 2, 1, 0, 1),
-        ('X', 1, 2, 6, 2),
+        ('W', 2, 6),
+        ('X', 2, 1, 4, 3),
+        ('X', 6, 1, 2, 3),
+        ('T', 1, 0, 3, 0),
+        ('T', 1, 0, 3, 1),
+        ('W', 7),
+        ('X', 7, 1, 2, 3),
+        ('X', 3, 1, 6, 2),
+        ('X', 2, 1, 7, 1),
         ('T', 0, 0, 3, 0),
         ('T', 0, 0, 3, 1),
-        ('T', 1, 0, 3, 0),
-        ('T', 1, 0, 3, 1),
-        ('W', 5, 3),
-        ('X', 5, 1, 0, 4),
-        ('X', 7, 1, 2, 2),
-        ('X', 3, 1, 6, 2),
-        ('X', 6, 1, 3, 1),
-        ('X', 3, 1, 0, 1),
-        ('H', 0, 4, 4, 1),
-        ('H', 0, 2, 4, 3),
-        ('H', 1, 2, 2, 2),
+        ('W', 1),
+        ('X', 1, 1, 4, 4),
+        ('H', 0, 4, 0, 1),
+        ('H', 0, 2, 0, 3),
+        ('H', 1, 2, 6, 2),
         ('T', 0, 0, 4, 0),
         ('T', 0, 0, 4, 1),
-        ('W', 4),
-        ('X', 4, 1, 0, 4),
-        ('X', 1, 3, 4, 2),
+        ('W', 0),
+        ('X', 0, 1, 4, 4),
+        ('X', 6, 2, 0, 2),
+        ('X', 5, 1, 0, 3),
+        ('H', 0, 0, 4, 4),
         ('H', 0, 0, 0, 4),
-        ('H', 0, 0, 4, 4),
     ),
     (
         ('F', 0, 3),
@@ -83,34 +83,34 @@
         ('F', 1, 1),
         ('O', 1, 3),
         ('T', 0, 3, 1, 1),
+        ('T', 0, 1, 1, 0),
         ('T', 1, 1, 1, 0),
-        ('T', 0, 1, 1, 0),
+        ('T', 0, 1, 1, 1),
         ('T', 1, 1, 1, 1),
-        ('T', 0, 1, 1, 1),
+        ('T', 0, 1, 2, 0),
+        ('O', 1, 1),
         ('T', 1, 1, 2, 0),
-        ('O', 1, 1),
-        ('T', 0, 1, 2, 0),
         ('O', 0, 1),
+        ('T', 0, 1, 2, 1),
         ('T', 1, 1, 2, 1),
-        ('T', 0, 1, 2, 1),
         ('T', 0, 1, 3, 0),
         ('T', 0, 1, 3, 1),
+        ('B', 0, 1, 3),
+        ('B', 0, 1, 2),
+        ('B', 1, 1, 2),
         ('B', 0, 1, 1),
         ('B', 1, 1, 1),
         ('B', 0, 3, 1),
-        ('B', 0, 1, 2),
-        ('B', 1, 1, 2),
-        ('B', 0, 1, 3),
-        ('H', 1, 3, 3, 1),
-        ('H', 0, 3, 4, 2),
-        ('H', 1, 1, 1, 3),
-        ('H', 0, 1, 4, 4),
+        ('H', 1, 3, 7, 1),
+        ('H', 0, 3, 0, 2),
+        ('H', 1, 1, 5, 3),
+        ('H', 0, 1, 0, 4),
     ),
 )
 
 
 def place(way, k):
-    return k if way else (ZS - k) % ZS
+    return 4 + k if way else 4 - k
 
 
 def kernel(
@@ -233,7 +233,7 @@
         left = weighted[pl.ds(first, count)].reshape(count * PER, ML)
         value = dot(left, rows_of(0, 0, lo, n))
         for i in range(count):
-            emit(value[i * PER : (i + 1) * PER], z, up(0, first + i), lo, n)
+            emit(value[i * PER : (i + 1) * PER], z, up(0, first + i - 4), lo, n)
 
     def run(e):
         slots[0] = 0
@@ -285,7 +285,7 @@
         drain(stage.at[pl.ds(0, 57 if e == 0 else 59), :, pl.ds(0, 2 * PER)], o_recv)
         for p in range(ZS):
             for place_z in range(ZS):
-                at = (place_z - p if p % 2 == 0 else p - place_z) % ZS
+                at = (4 + (place_z - p if p % 2 == 0 else p - place_z)) % ZS
                 o_ref[2 * p : 2 * p + 2, :, place_z * PER : (place_z + 1) * PER] = found[
                     2 * p : 2 * p + 2, :, at * PER : (at + 1) * PER
                 ]

time: 56.8 us -> 54.5 us (0.960)
  Pallas kernels: 54.8 us -> 52.3 us
    pallas_call x1, Pallas kernels: 54.8 us -> 52.3 us  [per_device(): pl.pallas_call(kernel, out_shape=jax.ShapeDtypeStruct((BANDL, OWN, CH), B...]
where the time goes in v6:
time: 54.5 us; the launch traced here: 54.1 us
  Pallas kernels  52.3 us (96%)
  local copies, waits for them, and re-layouts  1.86 us (3%)
    pallas_call x1, Pallas kernels, per_device(): pl.pallas_call(kernel, out_shape=jax.ShapeDtypeStruct((BANDL, OWN, CH), B...  52.3 us
    unnamed x3, local copies, waits for them, and re-layouts  1.86 us

profile of v6, /device:TPU:1, one launch (start us, length us, event | category | flops | bytes accessed | tf_op | source)
XLA Modules:
  0.0 54.1 jit_solution(13416195298592858108)
XLA Ops:
  0.0 0.0 copy-start
  0.0 0.9 %copy-done = f32[16,1152]{1,0:T(8,128)S(1)} copy-done((f32[16,1152]{1,0:T(8,128)S(1)}, f32[16,1152]{1,0:T(8,128)}, u32[]{:S(2)}) %copy-start) | copy-done | bytes 73752
  0.9 52.3 %cross.1 = bf16[16,32,1024]{2,1,0:T(8,128)(2,1)S(1)} custom-call(bf16[32,16,1152]{2,1,0:T(8,128)(2,1)} %x_hbm.1, f32[16,1152]{1,0:T(8,128)S(1)} %copy-done), custom_call_target="tpu_custom_call" | custom-call | flops 1207959552 | bytes 4194304 | tf_op jit(solution)/shard_map/cross/pallas_call | solution.py:302
  53.2 1.0 %copy.4 = bf16[16,32,1024]{2,1,0:T(8,128)(2,1)} copy(bf16[16,32,1024]{2,1,0:T(8,128)(2,1)S(1)} %cross.1) | data formatting | bytes 2097152
Async XLA Ops:
  0.0 0.9 %copy-start = (f32[16,1152]{1,0:T(8,128)S(1)}, f32[16,1152]{1,0:T(8,128)}, u32[]{:S(2)}) copy-start(f32[16,1152]{1,0:T(8,128)} %w_hbm.1) | copy-start | bytes 221188

commit v7 on v6

--- a/solution.py
+++ b/solution.py
@@ -16,95 +16,27 @@
 ML = 1152
 CH = 1024
 
-ORDER = (((0, 4), (0, 2), (1, 2), (0, 0)), ((0, 3), (1, 3), (0, 1), (1, 1)))
+ORDER = (((0, 4), (0, 2), (1, 2), (0, 0)), ((0, 3), (1, 3), (1, 1), (0, 1)))
 
 
 PLAN = (
     (
-        ('F', 0, 4),
-        ('F', 0, 2),
-        ('F', 1, 2),
-        ('F', 0, 0),
-        ('O', 0, 4),
-        ('T', 0, 2, 1, 0),
-        ('T', 1, 2, 1, 0),
-        ('O', 0, 2),
-        ('O', 1, 2),
-        ('T', 0, 2, 1, 1),
-        ('T', 1, 2, 1, 1),
-        ('O', 0, 0),
-        ('T', 0, 2, 2, 0),
-        ('T', 0, 2, 2, 1),
-        ('B', 0, 2, 1),
-        ('B', 1, 2, 1),
-        ('B', 0, 2, 2),
-        ('T', 0, 0, 1, 0),
-        ('T', 0, 0, 1, 1),
-        ('T', 1, 0, 1, 0),
-        ('T', 1, 0, 1, 1),
-        ('W', 3, 4, 5),
-        ('X', 3, 1, 4, 2),
-        ('X', 5, 1, 3, 2),
-        ('T', 0, 0, 2, 0),
-        ('T', 0, 0, 2, 1),
-        ('T', 1, 0, 2, 0),
-        ('T', 1, 0, 2, 1),
-        ('W', 2, 6),
-        ('X', 2, 1, 4, 3),
-        ('X', 6, 1, 2, 3),
-        ('T', 1, 0, 3, 0),
-        ('T', 1, 0, 3, 1),
-        ('W', 7),
-        ('X', 7, 1, 2, 3),
-        ('X', 3, 1, 6, 2),
-        ('X', 2, 1, 7, 1),
-        ('T', 0, 0, 3, 0),
-        ('T', 0, 0, 3, 1),
-        ('W', 1),
-        ('X', 1, 1, 4, 4),
-        ('H', 0, 4, 0, 1),
-        ('H', 0, 2, 0, 3),
-        ('H', 1, 2, 6, 2),
-        ('T', 0, 0, 4, 0),
-        ('T', 0, 0, 4, 1),
-        ('W', 0),
-        ('X', 0, 1, 4, 4),
-        ('X', 6, 2, 0, 2),
-        ('X', 5, 1, 0, 3),
-        ('H', 0, 0, 4, 4),
-        ('H', 0, 0, 0, 4),
+        ('F', 0, 4), ('F', 0, 2), ('F', 1, 2), ('F', 0, 0), ('O', 0, 4), ('T', 0, 2, 1, 0), ('T', 1, 2, 1, 0),
+        ('O', 0, 2), ('O', 1, 2), ('T', 0, 2, 1, 1), ('T', 1, 2, 1, 1), ('O', 0, 0), ('T', 0, 2, 2, 0),
+        ('T', 0, 2, 2, 1), ('B', 0, 2, 2), ('B', 0, 2, 1), ('B', 1, 2, 1), ('T', 0, 0, 1, 0), ('T', 0, 0, 1, 1),
+        ('T', 1, 0, 1, 0), ('T', 1, 0, 1, 1), ('W', 3, 4, 5), ('X', 3, 1, 4, 2), ('X', 5, 1, 3, 2), ('T', 0, 0, 2, 0),
+        ('T', 0, 0, 2, 1), ('T', 1, 0, 2, 0), ('T', 1, 0, 2, 1), ('W', 2, 6), ('X', 2, 1, 4, 3), ('X', 6, 1, 2, 3),
+        ('T', 1, 0, 3, 0), ('T', 1, 0, 3, 1), ('W', 7), ('X', 7, 1, 2, 3), ('X', 3, 1, 6, 2), ('X', 2, 1, 7, 1),
+        ('T', 0, 0, 3, 0), ('T', 0, 0, 3, 1), ('W', 1), ('X', 1, 1, 4, 4), ('T', 0, 0, 4, 0), ('T', 0, 0, 4, 1),
+        ('W', 0), ('X', 0, 1, 4, 4), ('X', 6, 2, 0, 2), ('X', 5, 1, 0, 3), ('H', 0, 4, 0, 1), ('H', 0, 2, 0, 3),
+        ('H', 1, 2, 6, 2), ('H', 0, 0, 4, 4), ('H', 0, 0, 0, 4),
     ),
     (
-        ('F', 0, 3),
-        ('F', 1, 3),
-        ('F', 0, 1),
-        ('O', 0, 3),
-        ('T', 0, 3, 1, 0),
-        ('F', 1, 1),
-        ('O', 1, 3),
-        ('T', 0, 3, 1, 1),
-        ('T', 0, 1, 1, 0),
-        ('T', 1, 1, 1, 0),
-        ('T', 0, 1, 1, 1),
-        ('T', 1, 1, 1, 1),
-        ('T', 0, 1, 2, 0),
-        ('O', 1, 1),
-        ('T', 1, 1, 2, 0),
-        ('O', 0, 1),
-        ('T', 0, 1, 2, 1),
-        ('T', 1, 1, 2, 1),
-        ('T', 0, 1, 3, 0),
-        ('T', 0, 1, 3, 1),
-        ('B', 0, 1, 3),
-        ('B', 0, 1, 2),
-        ('B', 1, 1, 2),
-        ('B', 0, 1, 1),
-        ('B', 1, 1, 1),
-        ('B', 0, 3, 1),
-        ('H', 1, 3, 7, 1),
-        ('H', 0, 3, 0, 2),
-        ('H', 1, 1, 5, 3),
-        ('H', 0, 1, 0, 4),
+        ('F', 0, 3), ('F', 1, 3), ('F', 0, 1), ('O', 0, 3), ('T', 0, 3, 1, 0), ('F', 1, 1), ('O', 1, 3),
+        ('T', 0, 3, 1, 1), ('T', 0, 1, 1, 0), ('T', 1, 1, 1, 0), ('T', 0, 1, 1, 1), ('T', 1, 1, 1, 1),
+        ('T', 0, 1, 2, 0), ('O', 1, 1), ('T', 1, 1, 2, 0), ('O', 0, 1), ('T', 0, 1, 2, 1), ('T', 1, 1, 2, 1),
+        ('T', 0, 1, 3, 0), ('T', 0, 1, 3, 1), ('B', 0, 1, 3), ('B', 0, 1, 2), ('B', 1, 1, 2), ('B', 0, 1, 1),
+        ('B', 1, 1, 1), ('B', 0, 3, 1), ('H', 1, 3, 7, 1), ('H', 0, 3, 0, 2), ('H', 1, 1, 5, 3), ('H', 0, 1, 0, 4),
     ),
 )
 

time: 54.5 us -> 54.3 us (level)
  no operation moved by 1% of the time
where the time goes in v7:
time: 54.3 us; the launch traced here: 54.1 us
  Pallas kernels  52.2 us (96%)
  local copies, waits for them, and re-layouts  1.86 us (3%)
    pallas_call x1, Pallas kernels, per_device(): pl.pallas_call(kernel, out_shape=jax.ShapeDtypeStruct((BANDL, OWN, CH), B...  52.2 us
    unnamed x3, local copies, waits for them, and re-layouts  1.86 us

profile of v7, /device:TPU:1, one launch (start us, length us, event | category | flops | bytes accessed | tf_op | source)
XLA Modules:
  0.0 54.1 jit_solution(5381847946249100550)
XLA Ops:
  0.0 0.0 copy-start
  0.0 0.9 %copy-done = f32[16,1152]{1,0:T(8,128)S(1)} copy-done((f32[16,1152]{1,0:T(8,128)S(1)}, f32[16,1152]{1,0:T(8,128)}, u32[]{:S(2)}) %copy-start) | copy-done | bytes 73752
  0.9 52.2 %cross.1 = bf16[16,32,1024]{2,1,0:T(8,128)(2,1)S(1)} custom-call(bf16[32,16,1152]{2,1,0:T(8,128)(2,1)} %x_hbm.1, f32[16,1152]{1,0:T(8,128)S(1)} %copy-done), custom_call_target="tpu_custom_call" | custom-call | flops 1207959552 | bytes 4194304 | tf_op jit(solution)/shard_map/cross/pallas_call | solution.py:234
  53.1 1.0 %copy.4 = bf16[16,32,1024]{2,1,0:T(8,128)(2,1)} copy(bf16[16,32,1024]{2,1,0:T(8,128)(2,1)S(1)} %cross.1) | data formatting | bytes 2097152
Async XLA Ops:
  0.0 0.9 %copy-start = (f32[16,1152]{1,0:T(8,128)S(1)}, f32[16,1152]{1,0:T(8,128)}, u32[]{:S(2)}) copy-start(f32[16,1152]{1,0:T(8,128)} %w_hbm.1) | copy-start | bytes 221188

commit v8 on v7

--- a/solution.py
+++ b/solution.py
@@ -28,7 +28,7 @@
         ('T', 0, 0, 2, 1), ('T', 1, 0, 2, 0), ('T', 1, 0, 2, 1), ('W', 2, 6), ('X', 2, 1, 4, 3), ('X', 6, 1, 2, 3),
         ('T', 1, 0, 3, 0), ('T', 1, 0, 3, 1), ('W', 7), ('X', 7, 1, 2, 3), ('X', 3, 1, 6, 2), ('X', 2, 1, 7, 1),
         ('T', 0, 0, 3, 0), ('T', 0, 0, 3, 1), ('W', 1), ('X', 1, 1, 4, 4), ('T', 0, 0, 4, 0), ('T', 0, 0, 4, 1),
-        ('W', 0), ('X', 0, 1, 4, 4), ('X', 6, 2, 0, 2), ('X', 5, 1, 0, 3), ('H', 0, 4, 0, 1), ('H', 0, 2, 0, 3),
+        ('W', 0), ('X', 0, 1, 4, 2), ('X', 0, 1, 6, 2), ('X', 6, 2, 0, 2), ('X', 5, 1, 0, 3), ('H', 0, 4, 0, 1), ('H', 0, 2, 0, 3),
         ('H', 1, 2, 6, 2), ('H', 0, 0, 4, 4), ('H', 0, 0, 0, 4),
     ),
     (

time: 54.3 us -> 54.5 us (level)
  no operation moved by 1% of the time
where the time goes in v8:
time: 54.5 us; the launch traced here: 54.3 us
  Pallas kernels  52.4 us (96%)
  local copies, waits for them, and re-layouts  1.86 us (3%)
    pallas_call x1, Pallas kernels, per_device(): pl.pallas_call(kernel, out_shape=jax.ShapeDtypeStruct((BANDL, OWN, CH), B...  52.4 us
    unnamed x3, local copies, waits for them, and re-layouts  1.86 us

profile of v8, /device:TPU:1, one launch (start us, length us, event | category | flops | bytes accessed | tf_op | source)
XLA Modules:
  0.0 54.3 jit_solution(10773604859989819413)
XLA Ops:
  0.0 0.0 copy-start
  0.0 0.9 %copy-done = f32[16,1152]{1,0:T(8,128)S(1)} copy-done((f32[16,1152]{1,0:T(8,128)S(1)}, f32[16,1152]{1,0:T(8,128)}, u32[]{:S(2)}) %copy-start) | copy-done | bytes 73752
  0.9 52.4 %cross.1 = bf16[16,32,1024]{2,1,0:T(8,128)(2,1)S(1)} custom-call(bf16[32,16,1152]{2,1,0:T(8,128)(2,1)} %x_hbm.1, f32[16,1152]{1,0:T(8,128)S(1)} %copy-done), custom_call_target="tpu_custom_call" | custom-call | flops 1207959552 | bytes 4194304 | tf_op jit(solution)/shard_map/cross/pallas_call | solution.py:234
  53.3 1.0 %copy.4 = bf16[16,32,1024]{2,1,0:T(8,128)(2,1)} copy(bf16[16,32,1024]{2,1,0:T(8,128)(2,1)S(1)} %cross.1) | data formatting | bytes 2097152
Async XLA Ops:
  0.0 0.9 %copy-start = (f32[16,1152]{1,0:T(8,128)S(1)}, f32[16,1152]{1,0:T(8,128)}, u32[]{:S(2)}) copy-start(f32[16,1152]{1,0:T(8,128)} %w_hbm.1) | copy-start | bytes 221188
